TPU v7x, 512 devices: a whole 4x8x8 slice. The times are simulated.
512 devices in a mesh: row: 32 (over x_hi, y, core), col: 16 (over x_lo, z).
Axes of the slice: x: 4 (x_hi: 2, x_lo: 2; x = x_hi * 2 + x_lo), y: 8, z: 8, core: 2. Of those that a mesh axis runs over, the one named last changes fastest.
Arguments:
- prior: bfloat16 [65536, 256], P(('row', 'col')), may hold values from 0.1 to 2
- inv_degree: float32 [65536], P(('row', 'col')), may hold values from 0.03125 to 0.125
- seed_rows: int32 [8192], P(('row', 'col')), may hold values from 0 to 127, as said below
- seed_scores: bfloat16 [8192, 256], P(('row', 'col')), may hold values from 0.1 to 2
- block_mask: int32 [36864, 128, 128], P(('row', 'col')), may hold values 0 or 1
- block_row: int32 [36864], P(('row', 'col')), may hold values from 0 to 31, as said below
- block_col: int32 [36864], P(('row', 'col')), may hold values from 0 to 15, as said below
- block_live: int32 [512], P(('row', 'col')), may hold values from 9 to 72, as said below
Outputs:
- labels: bfloat16 [65536, 256], P(('row', 'col'))
Inputs may be any that keep to these rules, and one draw needn't show every extreme that they name: `seed_rows`: within one device's 16 entries the indices are distinct. Within one device's 72 slots, the pairs (block_row, block_col) are distinct. `block_col`: see block_row. `block_live`: some device uses all 72 slots.
All inputs are finite; a program needn't handle non-finite values. No bound on the sum of `block_mask` on one device may be relied on, other than what follows from the above.
Results may differ from a plain program's by a relative error of at most 0.015.
Values may be sent and summed in bfloat16 or wider, within the bound.
A program may use at most 64 MiB of HBM per device.

v0:
```python
import jax
import jax.numpy as jnp
from jax import lax
from jax.sharding import PartitionSpec as P

ITERS = 2
MIX_RATE = 0.9


def local(prior, inv_degree, seed_rows, seed_scores, block_mask, block_row, block_col, block_live):
    docs_dev, width = prior.shape
    slots, side = (block_mask.shape[0], block_mask.shape[1])
    target_blocks = lax.axis_size("row") * docs_dev // side
    live = block_live[0]
    slot_ids = jnp.arange(slots, dtype=jnp.int32)
    weights = (block_mask * (slot_ids < live).astype(jnp.int32)[:, None, None]).astype(jnp.bfloat16)
    hits = (seed_rows[:, None] == jnp.arange(docs_dev, dtype=jnp.int32)[None, :]).astype(
        jnp.bfloat16
    )
    seeded = jnp.dot(hits.T, seed_scores, preferred_element_type=jnp.float32)
    covered = jnp.sum(hits.astype(jnp.float32), axis=0) > 0.5
    base = (1.0 - MIX_RATE) * prior.astype(jnp.float32)
    factor = MIX_RATE * inv_degree[:, None]
    labels = prior
    for step in range(ITERS):
        sources = lax.all_gather(labels, "col", axis=0, tiled=True)
        src_blocks = sources.reshape(-1, side, width)
        picked = jnp.take(src_blocks, block_col, axis=0)
        products = jnp.einsum("sij,sjl->sil", weights, picked, preferred_element_type=jnp.float32)
        summed = jnp.zeros((target_blocks, side, width), jnp.float32).at[block_row].add(products)
        summed = summed.reshape(target_blocks * side, width)
        sums = lax.psum_scatter(
            summed.astype(jnp.bfloat16), "row", scatter_dimension=0, tiled=True
        ).astype(jnp.float32)
        fresh = factor * sums + base
        labels = jnp.where(covered[:, None], seeded, fresh).astype(jnp.bfloat16)
    return labels


def solution(mesh):
    return jax.shard_map(
        local,
        mesh=mesh,
        in_specs=(
            P(("row", "col"), None),
            P(("row", "col")),
            P(("row", "col")),
            P(("row", "col"), None),
            P(("row", "col"), None, None),
            P(("row", "col")),
            P(("row", "col")),
            P(("row", "col")),
        ),
        out_specs=P(("row", "col"), None),
        check_vma=False,
    )
```

profile of v0, /device:TPU:16, one launch (start us, length us, event | category | flops | bytes accessed | tf_op | source)
XLA Modules:
  0.0 508.4 jit_solution(6479234486084292138)
XLA Ops:
  6.5 0.0 copy-start
  6.5 0.0 all-gather.3.cloned.1.call-start
  6.5 0.7 all-gather.3.cloned.1.call-update
  7.3 0.0 reduce-scatter.3.cloned.1.call-start
  8.0 0.7 compare_select_fusion
  8.6 0.7 compare_select_fusion.1
  9.3 0.7 compare_and_fusion
  9.9 76.6 %all-gather.3.cloned.1.call-done = bf16[2048,256]{1,0:T(8,128)(2,1)} async-done(((bf16[128,256]{1,0:T(8,128)(2,1)}), bf16[2048,256]{1,0:T(8,128)(2,1)}) %all-gather.3.cloned.1.call-update) | async-done | bytes 1048592 | tf_op jit(solution)/shard_map/all_gather | solution.py:26
  86.5 6.8 %gather_fusion = bf16[72,128,256]{2,1,0:T(8,128)(2,1)} fusion(bf16[16,128,256]{2,1,0:T(8,128)(2,1)} %bitcast.7, s32[1024]{0:T(1024)S(1)} %pad_clamp_fusion), kind=kCustom, calls=%fused_computation.clone | custom fusion | bytes 9437472 | tf_op jit(solution)/shard_map/jit(_take)/gather | solution.py:28
  93.3 8.9 %fusion.2 = f32[72,128,256]{2,1,0:T(8,128)} fusion(bf16[72,128,256]{2,1,0:T(8,128)(2,1)} %gather_fusion, pred[72]{0:T(512)(128)(4,1)S(1)} %get-tuple-element.8, s32[72,128,128]{2,1,0:T(8,128)} %param.14, s32[72]{0:T(128)S(1)} %get-tuple-element.9), kind=kOutput, calls=%fused_computation.6 | convolution fusion | flops 608698368 | bytes 18874728 | tf_op jit(solution)/shard_map/sij,sjl->sil/dot_general | solution.py:29
  102.2 2.6 broadcast.23.clone
  104.8 23.3 %scatter_fusion = f32[32,128,256]{2,1,0:T(8,128)} fusion(f32[32,128,256]{2,1,0:T(8,128)} %broadcast.23.clone, s32[72]{0:T(128)S(1)} %compare_select_fusion.1, f32[72,128,256]{2,1,0:T(8,128)} %fusion.2), kind=kCustom, calls=%fused_computation.2 | custom fusion | flops 2359296 | bytes 28311840 | tf_op jit(solution)/shard_map/scatter-add | solution.py:30
  128.1 0.0 copy-start.3
  128.1 0.0 copy-start.2
  128.1 0.0 copy-start.1
  128.1 3.8 convert_element_type.47
  131.9 0.0 reduce-scatter.3.cloned.1.call-update
  131.9 0.0 all-gather.5.cloned.1.call-start
  132.0 0.0 copy-done.3
  132.0 0.1 convert_reduce_fusion
  132.1 0.0 copy-done.2
  132.1 124.6 %reduce-scatter.3.cloned.1.call-done = bf16[128,256]{1,0:T(8,128)(2,1)} async-done(((bf16[4096,256]{1,0:T(8,128)(2,1)}), bf16[128,256]{1,0:T(8,128)(2,1)}) %reduce-scatter.3.cloned.1.call-update) | async-done | bytes 65552 | tf_op jit(solution)/shard_map/reduce_scatter | solution.py:32
  256.7 0.0 copy-done
  256.7 0.0 copy-done.1
  256.7 1.8 select_convert_fusion.1
  258.5 0.0 all-gather.5.cloned.1.call-update
  258.5 0.0 reduce-scatter.5.cloned.1.call-start
  258.5 71.6 %all-gather.5.cloned.1.call-done = bf16[2048,256]{1,0:T(8,128)(2,1)} async-done(((bf16[128,256]{1,0:T(8,128)(2,1)}), bf16[2048,256]{1,0:T(8,128)(2,1)}) %all-gather.5.cloned.1.call-update) | async-done | bytes 1048592 | tf_op jit(solution)/shard_map/all_gather | solution.py:26
  330.1 6.8 %gather_fusion.1 = bf16[72,128,256]{2,1,0:T(8,128)(2,1)} fusion(bf16[16,128,256]{2,1,0:T(8,128)(2,1)} %bitcast.8, s32[1024]{0:T(1024)S(1)} %pad_clamp_fusion), kind=kCustom, calls=%fused_computation.1.clone | custom fusion | bytes 9437472 | tf_op jit(solution)/shard_map/jit(_take)/gather | solution.py:28
  337.0 8.9 %fusion = f32[72,128,256]{2,1,0:T(8,128)} fusion(bf16[72,128,256]{2,1,0:T(8,128)(2,1)} %gather_fusion.1, pred[72]{0:T(512)(128)(4,1)S(1)} %get-tuple-element.8, s32[72,128,128]{2,1,0:T(8,128)} %param.14, s32[72]{0:T(128)S(1)} %get-tuple-element.9), kind=kOutput, calls=%fused_computation.4 | convolution fusion | flops 608698368 | bytes 18874728 | tf_op jit(solution)/shard_map/sij,sjl->sil/dot_general | solution.py:29
  345.8 2.6 broadcast.23
  348.4 23.3 %scatter_fusion.1 = f32[32,128,256]{2,1,0:T(8,128)} fusion(f32[32,128,256]{2,1,0:T(8,128)} %broadcast.23, s32[72]{0:T(128)S(1)} %compare_select_fusion.1, f32[72,128,256]{2,1,0:T(8,128)} %fusion), kind=kCustom, calls=%fused_computation.3 | custom fusion | flops 2359296 | bytes 28311840 | tf_op jit(solution)/shard_map/scatter-add | solution.py:30
  371.7 3.8 convert_element_type.52
  375.5 0.0 reduce-scatter.5.cloned.1.call-update
  375.5 124.8 %reduce-scatter.5.cloned.1.call-done = bf16[128,256]{1,0:T(8,128)(2,1)} async-done(((bf16[4096,256]{1,0:T(8,128)(2,1)}), bf16[128,256]{1,0:T(8,128)(2,1)}) %reduce-scatter.5.cloned.1.call-update) | async-done | bytes 65552 | tf_op jit(solution)/shard_map/reduce_scatter | solution.py:32
  500.3 1.6 select_convert_fusion
  (3 shorter events, 0.0 us)
Async XLA Ops:
  6.5 250.2 %copy-start = (bf16[16,256]{1,0:T(8,128)(2,1)S(1)}, bf16[16,256]{1,0:T(8,128)(2,1)}, u32[]{:S(2)}) copy-start(bf16[16,256]{1,0:T(8,128)(2,1)} %param.13) | copy-start | bytes 24580
  6.5 80.0 %all-gather.3.cloned.1.call-start = ((), (), s32[]{:S(2)}) async-start(), calls=%async_computation.2 | async-start | bytes 1114112 | tf_op jit(solution)/shard_map/all_gather | solution.py:26
  7.3 249.4 %reduce-scatter.3.cloned.1.call-start = ((), (), s32[]{:S(2)}) async-start(), calls=%async_computation.3 | async-start | bytes 2162688 | tf_op jit(solution)/shard_map/reduce_scatter | solution.py:32
  128.1 3.9 copy-start.3
  128.1 4.0 copy-start.2
  128.1 128.6 %copy-start.1 = (bf16[128,256]{1,0:T(8,128)(2,1)S(1)}, bf16[128,256]{1,0:T(8,128)(2,1)}, u32[]{:S(2)}) copy-start(bf16[128,256]{1,0:T(8,128)(2,1)} %param.10) | copy-start | bytes 196612
  131.9 198.2 %all-gather.5.cloned.1.call-start = ((), (), s32[]{:S(2)}) async-start(), calls=%async_computation.4 | async-start | bytes 1114112 | tf_op jit(solution)/shard_map/all_gather | solution.py:26
  258.5 241.8 %reduce-scatter.5.cloned.1.call-start = ((), (), s32[]{:S(2)}) async-start(), calls=%async_computation.5 | async-start | bytes 2162688 | tf_op jit(solution)/shard_map/reduce_scatter | solution.py:32
Sparse Core Ops, SparseCore 0:
  9.4 77.0 all-gather.2
  132.1 124.5 reduce-scatter.2
  259.0 71.0 all-gather.4
  375.6 124.6 reduce-scatter.4
where the time goes:
time: 509 us; the launch traced here: 508 us
  waiting for transfers between devices  398 us (78%)
  other arithmetic  57.9 us (11%)
  matrix products  19.5 us (4%)
  local copies, waits for them, and re-layouts  18.8 us (4%)
  between operations  13.8 us (3%)
    reduce_scatter x2, waiting for transfers between devices, local(): lax.psum_scatter(summed.astype(jnp.bfloat16), 'row', scatter_dimension=0,...  249 us
    all_gather x2, waiting for transfers between devices, local(): sources = lax.all_gather(labels, 'col', axis=0, tiled=True)  148 us
    scatter-add x2, other arithmetic, local(): jnp.zeros((target_blocks, side, width), jnp.float32).at[block_row]  46.6 us
    dot_general x2, matrix products, local(): jnp.einsum('sij,sjl->sil', weights, picked, preferred_element_type=jnp.fl...  17.7 us
    gather x2, local copies, waits for them, and re-layouts, local(): picked = jnp.take(src_blocks, block_col, axis=0)  13.6 us
  transfers between devices with their start and end apart: 4, of which 4 were waited for; matrix products, arithmetic and copies ran while one was open for 0% of the time, Pallas kernels for 0%

commit v1 on v0

--- a/solution.py
+++ b/solution.py
@@ -23,7 +23,10 @@
     factor = MIX_RATE * inv_degree[:, None]
     labels = prior
     for step in range(ITERS):
-        sources = lax.all_gather(labels, "col", axis=0, tiled=True)
+        size = lax.axis_size("col")
+        shards = jnp.stack([labels for _ in range(size)])
+        shards = lax.all_to_all(shards, "col", split_axis=0, concat_axis=0)
+        sources = jnp.concatenate(shards, axis=0)
         src_blocks = sources.reshape(-1, side, width)
         picked = jnp.take(src_blocks, block_col, axis=0)
         products = jnp.einsum("sij,sjl->sil", weights, picked, preferred_element_type=jnp.float32)

time: 509 us -> 423 us (0.83)
  waiting for transfers between devices: 398 us -> 273 us
  blocking collectives: 0 us -> 29.1 us
  starting transfers between devices: 0.12 us -> 11.4 us
    all_gather x2 -> x0, waiting for transfers between devices: 148 us -> none  [local(): sources = lax.all_gather(labels, 'col', axis=0, tiled=True)]
    all_to_all x0 -> x1, blocking collectives: none -> 29.1 us  [local(): shards = lax.all_to_all(shards, 'col', split_axis=0, concat_axis=0)]
    all_to_all x0 -> x1, waiting for transfers between devices: none -> 24.4 us  [local(): shards = lax.all_to_all(shards, 'col', split_axis=0, concat_axis=0)]
    all_to_all x0 -> x1, starting transfers between devices: none -> 11.3 us  [local(): shards = lax.all_to_all(shards, 'col', split_axis=0, concat_axis=0)]
  transfers between devices with their start and end apart: 4 -> 3, of which waited for: 4 -> 3; matrix products, arithmetic and copies ran while one was open for 0% -> 0% of each run, Pallas kernels for 0% -> 0%
where the time goes in v1:
time: 423 us; the launch traced here: 422 us
  waiting for transfers between devices  273 us (65%)
  other arithmetic  58.1 us (14%)
  blocking collectives  29.1 us (7%)
  matrix products  18.8 us (4%)
  local copies, waits for them, and re-layouts  18.3 us (4%)
  between operations  14.1 us (3%)
  starting transfers between devices  11.4 us (3%)
    reduce_scatter x2, waiting for transfers between devices, local(): lax.psum_scatter(summed.astype(jnp.bfloat16), 'row', scatter_dimension=0,...  248 us
    scatter-add x2, other arithmetic, local(): jnp.zeros((target_blocks, side, width), jnp.float32).at[block_row]  46.7 us
    all_to_all x1, blocking collectives, local(): shards = lax.all_to_all(shards, 'col', split_axis=0, concat_axis=0)  29.1 us
    all_to_all x1, waiting for transfers between devices, local(): shards = lax.all_to_all(shards, 'col', split_axis=0, concat_axis=0)  24.4 us
    dot_general x2, matrix products, local(): jnp.einsum('sij,sjl->sil', weights, picked, preferred_element_type=jnp.fl...  17.7 us
    all_to_all x1, starting transfers between devices, local(): shards = lax.all_to_all(shards, 'col', split_axis=0, concat_axis=0)  11.3 us
    gather x2, local copies, waits for them, and re-layouts, local(): picked = jnp.take(src_blocks, block_col, axis=0)  11.2 us
  transfers between devices with their start and end apart: 3, of which 3 were waited for; matrix products, arithmetic and copies ran while one was open for 0% of the time, Pallas kernels for 0%

profile of v1, /device:TPU:16, one launch (start us, length us, event | category | flops | bytes accessed | tf_op | source)
XLA Modules:
  0.0 422.5 jit_solution(10866430082161223295)
XLA Ops:
  6.5 0.0 copy-start
  6.5 1.9 stack.4
  8.5 11.3 %all-to-all-start = ((bf16[16,128,256]{2,1,0:T(8,128)(2,1)}), bf16[16,128,256]{2,1,0:T(8,128)(2,1)S(1)}, u32[]{:S(2)}, u32[]{:S(2)}) async-start(bf16[16,128,256]{2,1,0:T(8,128)(2,1)} %stack.4), calls=%async_computation | async-start | bytes 2097152 | tf_op jit(solution)/shard_map/all_to_all | solution.py:28
  19.8 0.0 reduce-scatter.3.cloned.1.call-start
  20.5 0.7 compare_select_fusion
  21.2 0.7 compare_select_fusion.1
  21.9 0.7 compare_and_fusion
  22.5 24.4 %all-to-all-done = bf16[16,128,256]{2,1,0:T(8,128)(2,1)S(1)} async-done(((bf16[16,128,256]{2,1,0:T(8,128)(2,1)}), bf16[16,128,256]{2,1,0:T(8,128)(2,1)S(1)}, u32[]{:S(2)}, u32[]{:S(2)}) %all-to-all-start) | async-done | bytes 1048608 | tf_op jit(solution)/shard_map/all_to_all | solution.py:28
  46.9 5.6 %gather_fusion = bf16[72,128,256]{2,1,0:T(8,128)(2,1)} fusion(bf16[16,128,256]{2,1,0:T(8,128)(2,1)S(1)} %all-to-all-done, s32[1024]{0:T(1024)S(1)} %pad_clamp_fusion), kind=kCustom, calls=%fused_computation.clone | custom fusion | bytes 9437472 | tf_op jit(solution)/shard_map/jit(_take)/gather | solution.py:31
  52.5 8.9 %fusion.2 = f32[72,128,256]{2,1,0:T(8,128)} fusion(bf16[72,128,256]{2,1,0:T(8,128)(2,1)} %gather_fusion, pred[72]{0:T(512)(128)(4,1)S(1)} %get-tuple-element.8, s32[72,128,128]{2,1,0:T(8,128)} %param.14, s32[72]{0:T(128)S(1)} %get-tuple-element.9), kind=kOutput, calls=%fused_computation.6 | convolution fusion | flops 608698368 | bytes 18874728 | tf_op jit(solution)/shard_map/sij,sjl->sil/dot_general | solution.py:32
  61.4 2.6 broadcast.27.clone
  63.9 23.4 %scatter_fusion = f32[32,128,256]{2,1,0:T(8,128)} fusion(f32[32,128,256]{2,1,0:T(8,128)} %broadcast.27.clone, s32[72]{0:T(128)S(1)} %compare_select_fusion.1, f32[72,128,256]{2,1,0:T(8,128)} %fusion.2), kind=kCustom, calls=%fused_computation.2 | custom fusion | flops 2359296 | bytes 28311840 | tf_op jit(solution)/shard_map/scatter-add | solution.py:33
  87.3 0.0 copy-start.3
  87.3 0.0 copy-start.2
  87.3 0.0 copy-start.1
  87.3 3.9 convert_element_type.47
  91.1 0.0 reduce-scatter.3.cloned.1.call-update
  91.2 0.0 reduce-scatter.5.cloned.1.call-start
  91.2 0.0 copy-done.3
  91.2 0.1 convert_reduce_fusion
  91.3 0.0 copy-done.2
  91.3 124.8 %reduce-scatter.3.cloned.1.call-done = bf16[128,256]{1,0:T(8,128)(2,1)} async-done(((bf16[4096,256]{1,0:T(8,128)(2,1)}), bf16[128,256]{1,0:T(8,128)(2,1)}) %reduce-scatter.3.cloned.1.call-update) | async-done | bytes 65552 | tf_op jit(solution)/shard_map/reduce_scatter | solution.py:35
  216.2 0.0 copy-done
  216.2 0.0 copy-done.1
  216.2 1.1 select_convert_fusion.1
  217.3 0.1 stack.5
  217.4 29.1 %all_to_all.10 = bf16[16,128,256]{2,1,0:T(8,128)(2,1)S(1)} all-to-all(bf16[16,128,256]{2,1,0:T(8,128)(2,1)S(1)} %stack.5), channel_id=1, replica_groups=mesh['row'=32,'col'=16] {'col'}, dimensions={0} | all-to-all | bytes 2097152 | tf_op jit(solution)/shard_map/all_to_all | solution.py:28
  246.5 5.6 %gather_fusion.1 = bf16[72,128,256]{2,1,0:T(8,128)(2,1)} fusion(bf16[16,128,256]{2,1,0:T(8,128)(2,1)S(1)} %all_to_all.10, s32[1024]{0:T(1024)S(1)} %pad_clamp_fusion), kind=kCustom, calls=%fused_computation.1.clone | custom fusion | bytes 9437472 | tf_op jit(solution)/shard_map/jit(_take)/gather | solution.py:31
  252.1 8.9 %fusion = f32[72,128,256]{2,1,0:T(8,128)} fusion(bf16[72,128,256]{2,1,0:T(8,128)(2,1)} %gather_fusion.1, pred[72]{0:T(512)(128)(4,1)S(1)} %get-tuple-element.8, s32[72,128,128]{2,1,0:T(8,128)} %param.14, s32[72]{0:T(128)S(1)} %get-tuple-element.9), kind=kOutput, calls=%fused_computation.4 | convolution fusion | flops 608698368 | bytes 18874728 | tf_op jit(solution)/shard_map/sij,sjl->sil/dot_general | solution.py:32
  260.9 2.6 broadcast.27
  263.5 23.4 %scatter_fusion.1 = f32[32,128,256]{2,1,0:T(8,128)} fusion(f32[32,128,256]{2,1,0:T(8,128)} %broadcast.27, s32[72]{0:T(128)S(1)} %compare_select_fusion.1, f32[72,128,256]{2,1,0:T(8,128)} %fusion), kind=kCustom, calls=%fused_computation.3 | custom fusion | flops 2359296 | bytes 28311840 | tf_op jit(solution)/shard_map/scatter-add | solution.py:33
  286.8 3.8 convert_element_type.52
  290.7 0.0 reduce-scatter.5.cloned.1.call-update
  290.7 123.4 %reduce-scatter.5.cloned.1.call-done = bf16[128,256]{1,0:T(8,128)(2,1)} async-done(((bf16[4096,256]{1,0:T(8,128)(2,1)}), bf16[128,256]{1,0:T(8,128)(2,1)}) %reduce-scatter.5.cloned.1.call-update) | async-done | bytes 65552 | tf_op jit(solution)/shard_map/reduce_scatter | solution.py:35
  414.1 1.6 select_convert_fusion
  (3 shorter events, 0.0 us)
Async XLA Ops:
  6.5 209.6 %copy-start = (bf16[16,256]{1,0:T(8,128)(2,1)S(1)}, bf16[16,256]{1,0:T(8,128)(2,1)}, u32[]{:S(2)}) copy-start(bf16[16,256]{1,0:T(8,128)(2,1)} %param.13) | copy-start | bytes 24580
  8.5 38.4 %all-to-all-start = ((bf16[16,128,256]{2,1,0:T(8,128)(2,1)}), bf16[16,128,256]{2,1,0:T(8,128)(2,1)S(1)}, u32[]{:S(2)}, u32[]{:S(2)}) async-start(bf16[16,128,256]{2,1,0:T(8,128)(2,1)} %stack.4), calls=%async_computation | async-start | bytes 2097152 | tf_op jit(solution)/shard_map/all_to_all | solution.py:28
  19.8 196.3 %reduce-scatter.3.cloned.1.call-start = ((), (), s32[]{:S(2)}) async-start(), calls=%async_computation.4 | async-start | bytes 2162688 | tf_op jit(solution)/shard_map/reduce_scatter | solution.py:35
  87.3 3.9 copy-start.3
  87.3 4.1 copy-start.2
  87.3 128.9 %copy-start.1 = (bf16[128,256]{1,0:T(8,128)(2,1)S(1)}, bf16[128,256]{1,0:T(8,128)(2,1)}, u32[]{:S(2)}) copy-start(bf16[128,256]{1,0:T(8,128)(2,1)} %param.10) | copy-start | bytes 196612
  91.2 322.9 %reduce-scatter.5.cloned.1.call-start = ((), (), s32[]{:S(2)}) async-start(), calls=%async_computation.5 | async-start | bytes 2162688 | tf_op jit(solution)/shard_map/reduce_scatter | solution.py:35
Sparse Core Ops, SparseCore 0:
  91.3 124.8 reduce-scatter.2
  290.8 123.2 reduce-scatter.4
